TPU v7x, 32 devices: a whole 2x2x4 slice. The times are simulated.
32 devices in a mesh: dp: 8 (over z, y), chan: 4 (over x, core).
Axes of the slice: x: 2, y: 2, z: 4, core: 2. Of those that a mesh axis runs over, the one named last changes fastest.
Arguments:
- mel: bfloat16 [16, 2816, 80], P('dp', 'chan'), may hold values from -6 to 6
- lang_group: int32 [16], P('dp'), may hold values from 0 to 15
- clip_count: int32 [8], replicated, may hold values from 1 to 2, as said below
- conv_one: bfloat16 [240, 768], P(None, 'chan'), may hold values from -0.375 to 0.375
- conv_one_bias: bfloat16 [768], P('chan'), may hold values from -1.796875 to 1.796875
- conv_two: bfloat16 [3, 768, 768], P(None, 'chan'), may hold values from -0.125 to 0.125
- conv_two_bias: bfloat16 [768], replicated, may hold values from -1.796875 to 1.796875
- lang_table: bfloat16 [16, 768], replicated, may hold values from -3 to 3
- ln_one_gain: bfloat16 [768], replicated, may hold values from 0.5 to 1.5
- ln_one_bias: bfloat16 [768], replicated, may hold values from -1.796875 to 1.796875
- w_qkv: bfloat16 [768, 2304], P('chan'), may hold values from -0.3125 to 0.3125
- q_bias: bfloat16 [768], replicated, may hold values from -1.796875 to 1.796875
- v_bias: bfloat16 [768], replicated, may hold values from -1.796875 to 1.796875
- w_out: bfloat16 [768, 768], P('chan'), may hold values from -0.875 to 0.875
- out_bias: bfloat16 [768], replicated, may hold values from -1.796875 to 1.796875
- ln_two_gain: bfloat16 [768], replicated, may hold values from 0.5 to 1.5
- ln_two_bias: bfloat16 [768], replicated, may hold values from -1.796875 to 1.796875
- w_fc_one: bfloat16 [768, 3072], P('chan'), may hold values from -0.21875 to 0.21875
- fc_one_bias: bfloat16 [3072], replicated, may hold values from -1.796875 to 1.796875
- w_fc_two: bfloat16 [3072, 768], P('chan'), may hold values from -0.109375 to 0.109375
- fc_two_bias: bfloat16 [768], replicated, may hold values from -1.796875 to 1.796875
- grad_out: bfloat16 [16, 1408, 768], P('dp', 'chan'), may hold values from -6 to 6
Outputs:
- encoded: bfloat16 [16, 1408, 768], P('dp', 'chan')
- mel_grad: float32 [16, 2816, 80], P('dp', 'chan')
- conv_one_grad: float32 [240, 768], P(None, 'chan')
- conv_one_bias_grad: float32 [768], P('chan')
- conv_two_grad: float32 [3, 768, 768], P(None, 'chan')
- conv_two_bias_grad: float32 [768], replicated
- lang_table_grad: float32 [16, 768], replicated
- ln_one_gain_grad: float32 [768], replicated
- ln_one_bias_grad: float32 [768], replicated
- w_qkv_grad: float32 [768, 2304], P('chan')
- q_bias_grad: float32 [768], replicated
- v_bias_grad: float32 [768], replicated
- w_out_grad: float32 [768, 768], P('chan')
- out_bias_grad: float32 [768], replicated
- ln_two_gain_grad: float32 [768], replicated
- ln_two_bias_grad: float32 [768], replicated
- w_fc_one_grad: float32 [768, 3072], P('chan')
- fc_one_bias_grad: float32 [3072], replicated
- w_fc_two_grad: float32 [3072, 768], P('chan')
- fc_two_bias_grad: float32 [768], replicated
Inputs may be any that keep to these rules, and one draw needn't show every extreme that they name: Slot s of index i of dp holds a live clip when s < clip_count[i]; some index has 2 live clips and some has 1.
All inputs are finite; a program needn't handle non-finite values.
Results may differ from a plain program's by a relative error of at most 0.02.
Values may be sent and summed in bfloat16 or wider, within the bound.
No kernel may reach another device: no remote copies, remote signals or barrier semaphores. Data moves between devices by JAX's collectives and lax.ppermute only.
A program may use at most 320 MiB of HBM per device.

v0:
```python
import math

import jax
import jax.numpy as jnp
from jax import lax
from jax.sharding import PartitionSpec as P

HEAD_DIM = 64


def gelu_exact(inputs):
    return jax.nn.gelu(inputs, approximate=False)


def gelu_back(inputs, cotangent):
    return jax.vjp(gelu_exact, inputs)[1](cotangent)[0]


def layer_norm(inputs, gain_vec, shift_vec):
    row_mean = jnp.mean(inputs, axis=-1, keepdims=True)
    centered = inputs - row_mean
    variance = jnp.mean(centered * centered, axis=-1, keepdims=True)
    return centered * lax.rsqrt(variance + 1e-05) * gain_vec + shift_vec


def norm_back(inputs, gain_vec, shift_vec, cotangent):
    return jax.vjp(layer_norm, inputs, gain_vec, shift_vec)[1](cotangent)


def positions(frame_count, model_width, first_frame):
    increment = math.log(10000.0) / (model_width // 2 - 1)
    inverse = jnp.exp(-increment * jnp.arange(model_width // 2, dtype=jnp.float32))
    angles = (first_frame + jnp.arange(frame_count)).astype(jnp.float32)[:, None] * inverse[None, :]
    return jnp.concatenate([jnp.sin(angles), jnp.cos(angles)], axis=1)


def cols_three(frames):
    length = frames.shape[1] - 2
    return jnp.concatenate(
        [frames[:, 0:length], frames[:, 1 : length + 1], frames[:, 2 : length + 2]], axis=2
    )


def taps_two(frames):
    length = (frames.shape[1] - 1) // 2
    return jnp.concatenate(
        [
            frames[:, 0 : 2 * length : 2],
            frames[:, 1 : 2 * length : 2],
            frames[:, 2 : 2 * length + 1 : 2],
        ],
        axis=2,
    )


def taps_back(grads):
    channels = grads.shape[2] // 3
    first_tap = grads[:, :, 0:channels]
    mid_tap = grads[:, :, channels : 2 * channels]
    last_tap = grads[:, :, 2 * channels :]
    following = jnp.pad(first_tap[:, 1:], ((0, 0), (0, 1), (0, 0))) + last_tap
    return jnp.stack([mid_tap, following], axis=2).reshape(
        grads.shape[0], 2 * grads.shape[1], channels
    )


def cols_back(grads):
    channels = grads.shape[2] // 3
    length = grads.shape[1] - 2
    return (
        grads[:, 2 : length + 2, 0:channels]
        + grads[:, 1 : length + 1, channels : 2 * channels]
        + grads[:, 0:length, 2 * channels :]
    )


def dot_rows(left, right):
    return lax.dot_general(
        left, right, (((2,), (0,)), ((), ())), preferred_element_type=jnp.float32
    )


def dot_trans(left, right):
    return lax.dot_general(
        left, right, (((left.ndim - 1,), (1,)), ((), ())), preferred_element_type=jnp.float32
    )


def outer_sum(left, right):
    return lax.dot_general(
        left, right, (((0,), (0,)), ((), ())), preferred_element_type=jnp.float32
    )


def attend(queries, key_rows, value_rows, score_scale):
    scores = (
        jnp.einsum("qhd,khd->hqk", queries, key_rows, preferred_element_type=jnp.float32)
        * score_scale
    )
    row_top = jnp.max(scores, axis=-1, keepdims=True)
    row_total = jnp.sum(jnp.exp(scores - row_top), axis=-1, keepdims=True)
    log_total = row_top + jnp.log(row_total)
    soft_probs = jnp.exp(scores - log_total).astype(jnp.bfloat16)
    attended = jnp.einsum(
        "hqk,khd->qhd", soft_probs, value_rows, preferred_element_type=jnp.float32
    )
    return (attended.astype(jnp.bfloat16), log_total)


def attend_back(queries, key_rows, value_rows, log_total, grad_att, score_scale):
    scores = (
        jnp.einsum("qhd,khd->hqk", queries, key_rows, preferred_element_type=jnp.float32)
        * score_scale
    )
    soft_probs = jnp.exp(scores - log_total)
    grad_probs = jnp.einsum(
        "qhd,khd->hqk", grad_att, value_rows, preferred_element_type=jnp.float32
    )
    inner = jnp.sum(soft_probs * grad_probs, axis=-1, keepdims=True)
    grad_scores = (soft_probs * (grad_probs - inner)).astype(jnp.bfloat16)
    grad_queries = (
        jnp.einsum("hqk,khd->qhd", grad_scores, key_rows, preferred_element_type=jnp.float32)
        * score_scale
    )
    grad_keys = (
        jnp.einsum("hqk,qhd->khd", grad_scores, queries, preferred_element_type=jnp.float32)
        * score_scale
    )
    grad_values = jnp.einsum(
        "hqk,qhd->khd",
        soft_probs.astype(jnp.bfloat16),
        grad_att,
        preferred_element_type=jnp.float32,
    )
    return (grad_queries, grad_keys, grad_values)


def on_device(
    mel,
    lang_group,
    clip_count,
    conv_one,
    conv_one_bias,
    conv_two,
    conv_two_bias,
    lang_table,
    ln_one_gain,
    ln_one_bias,
    w_qkv,
    q_bias,
    v_bias,
    w_out,
    out_bias,
    ln_two_gain,
    ln_two_bias,
    w_fc_one,
    fc_one_bias,
    w_fc_two,
    fc_two_bias,
    grad_out,
):
    slot_count = grad_out.shape[0]
    own_frames = grad_out.shape[1]
    model_width = grad_out.shape[2]
    chan_index = lax.axis_index("chan")
    all_frames = own_frames * lax.axis_size("chan")
    head_count = model_width // HEAD_DIM
    score_scale = HEAD_DIM ** (-0.5)
    live_mask = (jnp.arange(slot_count) < clip_count[lax.axis_index("dp")]).astype(jnp.float32)
    qkv_full, out_full, one_full, two_full = (
        lax.all_gather(w_qkv, "chan", axis=0, tiled=True),
        lax.all_gather(w_out, "chan", axis=0, tiled=True),
        lax.all_gather(w_fc_one, "chan", axis=0, tiled=True),
        lax.all_gather(w_fc_two, "chan", axis=0, tiled=True),
    )
    mel_all = lax.all_gather(mel, "chan", axis=1, tiled=True)
    mel_cols = cols_three(jnp.pad(mel_all, ((0, 0), (1, 1), (0, 0))))
    pre_one = dot_rows(mel_cols, conv_one) + conv_one_bias.astype(jnp.float32)
    hid_one = gelu_exact(pre_one).astype(jnp.bfloat16)
    hid_taps = taps_two(jnp.pad(hid_one, ((0, 0), (1, 0), (0, 0))))
    stem_sum = lax.psum_scatter(
        dot_rows(hid_taps, conv_two.reshape(-1, model_width)),
        "chan",
        scatter_dimension=1,
        tiled=True,
    )
    pre_two = stem_sum + conv_two_bias.astype(jnp.float32)
    lang_hot = (lang_group[:, None] == jnp.arange(lang_table.shape[0])[None, :]).astype(jnp.float32)
    lang_rows = jnp.dot(lang_hot, lang_table.astype(jnp.float32), precision=lax.Precision.HIGHEST)
    place_rows = positions(own_frames, model_width, chan_index * own_frames)
    stem_out = gelu_exact(pre_two) + place_rows[None] + lang_rows[:, None, :]
    gain_one = ln_one_gain.astype(jnp.float32)
    shift_one = ln_one_bias.astype(jnp.float32)
    gain_two = ln_two_gain.astype(jnp.float32)
    shift_two = ln_two_bias.astype(jnp.float32)
    stem_rows = stem_out.reshape(-1, model_width)
    normed = layer_norm(stem_rows, gain_one, shift_one).astype(jnp.bfloat16)
    qkv_shift = jnp.concatenate(
        [
            q_bias.astype(jnp.float32),
            jnp.zeros((model_width,), jnp.float32),
            v_bias.astype(jnp.float32),
        ]
    )
    packed = (jnp.dot(normed, qkv_full, preferred_element_type=jnp.float32) + qkv_shift).astype(
        jnp.bfloat16
    )
    queries = packed[:, 0:model_width].reshape(slot_count, own_frames, head_count, HEAD_DIM)
    key_all, value_all = (
        lax.all_gather(
            packed[:, model_width : 2 * model_width].reshape(slot_count, own_frames, model_width),
            "chan",
            axis=1,
            tiled=True,
        ),
        lax.all_gather(
            packed[:, 2 * model_width :].reshape(slot_count, own_frames, model_width),
            "chan",
            axis=1,
            tiled=True,
        ),
    )
    key_heads = key_all.reshape(slot_count, all_frames, head_count, HEAD_DIM)
    value_heads = value_all.reshape(slot_count, all_frames, head_count, HEAD_DIM)
    attended, log_total = lax.map(
        lambda bundle: attend(bundle[0], bundle[1], bundle[2], score_scale),
        (queries, key_heads, value_heads),
    )
    attended_rows = attended.reshape(-1, model_width)
    branch = jnp.dot(attended_rows, out_full, preferred_element_type=jnp.float32) + out_bias.astype(
        jnp.float32
    )
    residual = stem_rows + branch
    normed_two = layer_norm(residual, gain_two, shift_two).astype(jnp.bfloat16)
    upper_pre = jnp.dot(
        normed_two, one_full, preferred_element_type=jnp.float32
    ) + fc_one_bias.astype(jnp.float32)
    active = gelu_exact(upper_pre).astype(jnp.bfloat16)
    mlp_out = jnp.dot(active, two_full, preferred_element_type=jnp.float32) + fc_two_bias.astype(
        jnp.float32
    )
    encoded = (
        (residual + mlp_out).reshape(slot_count, own_frames, model_width) * live_mask[:, None, None]
    ).astype(jnp.bfloat16)
    grad_rows = (grad_out.astype(jnp.float32) * live_mask[:, None, None]).reshape(-1, model_width)
    grad_mlp = grad_rows.astype(jnp.bfloat16)
    grad_two = outer_sum(active, grad_mlp)
    grad_two_shift = jnp.sum(grad_mlp.astype(jnp.float32), axis=0)
    grad_active = dot_trans(grad_mlp, two_full)
    grad_upper = gelu_back(upper_pre, grad_active).astype(jnp.bfloat16)
    grad_one = outer_sum(normed_two, grad_upper)
    grad_one_shift = jnp.sum(grad_upper.astype(jnp.float32), axis=0)
    grad_normed_two = dot_trans(grad_upper, one_full)
    grad_res_norm, grad_gain_two, grad_shift_two = norm_back(
        residual, gain_two, shift_two, grad_normed_two
    )
    grad_residual = grad_rows + grad_res_norm
    grad_branch = grad_residual.astype(jnp.bfloat16)
    grad_out_proj = outer_sum(attended_rows, grad_branch)
    grad_out_shift = jnp.sum(grad_branch.astype(jnp.float32), axis=0)
    grad_att = (
        dot_trans(grad_branch, out_full)
        .astype(jnp.bfloat16)
        .reshape(slot_count, own_frames, head_count, HEAD_DIM)
    )
    grad_q, grad_k_all, grad_v_all = lax.map(
        lambda bundle: attend_back(
            bundle[0], bundle[1], bundle[2], bundle[3], bundle[4], score_scale
        ),
        (queries, key_heads, value_heads, log_total, grad_att),
    )
    grad_keys, grad_values = (
        lax.psum_scatter(
            grad_k_all.reshape(slot_count, all_frames, model_width).astype(jnp.bfloat16),
            "chan",
            scatter_dimension=1,
            tiled=True,
        ).astype(jnp.float32),
        lax.psum_scatter(
            grad_v_all.reshape(slot_count, all_frames, model_width).astype(jnp.bfloat16),
            "chan",
            scatter_dimension=1,
            tiled=True,
        ).astype(jnp.float32),
    )
    grad_packed = jnp.concatenate(
        [
            grad_q.reshape(-1, model_width),
            grad_keys.reshape(-1, model_width),
            grad_values.reshape(-1, model_width),
        ],
        axis=1,
    ).astype(jnp.bfloat16)
    grad_qkv = outer_sum(normed, grad_packed)
    grad_q_shift = jnp.sum(grad_packed[:, 0:model_width].astype(jnp.float32), axis=0)
    grad_v_shift = jnp.sum(grad_packed[:, 2 * model_width :].astype(jnp.float32), axis=0)
    grad_normed = dot_trans(grad_packed, qkv_full)
    grad_stem_norm, grad_gain_one, grad_shift_one = norm_back(
        stem_rows, gain_one, shift_one, grad_normed
    )
    grad_stem = (grad_residual + grad_stem_norm).reshape(slot_count, own_frames, model_width)
    grad_lang = jnp.dot(lang_hot.T, jnp.sum(grad_stem, axis=1), precision=lax.Precision.HIGHEST)
    grad_pre_two = gelu_back(pre_two, grad_stem).astype(jnp.bfloat16)
    grad_conv_two_shift = jnp.sum(grad_pre_two.astype(jnp.float32), axis=(0, 1))
    grad_frames_all = lax.all_gather(grad_pre_two, "chan", axis=1, tiled=True)
    grad_taps = dot_trans(grad_frames_all, conv_two.reshape(-1, model_width))
    grad_hid = taps_back(grad_taps)
    grad_pre_one = gelu_back(pre_one, grad_hid).astype(jnp.bfloat16)
    grad_conv_two = outer_sum(
        hid_taps.reshape(-1, hid_taps.shape[2]), grad_frames_all.reshape(-1, model_width)
    ).reshape(conv_two.shape)
    grad_conv_one = outer_sum(
        mel_cols.reshape(-1, mel_cols.shape[2]), grad_pre_one.reshape(-1, grad_pre_one.shape[2])
    )
    grad_conv_one_shift = jnp.sum(grad_pre_one.astype(jnp.float32), axis=(0, 1))
    mel_terms = cols_back(jnp.pad(dot_trans(grad_pre_one, conv_one), ((0, 0), (1, 1), (0, 0))))
    mel_grad = lax.psum_scatter(
        mel_terms.astype(jnp.bfloat16), "chan", scatter_dimension=1, tiled=True
    ).astype(jnp.float32)
    qkv_share, out_share, one_share, two_share = (
        lax.psum_scatter(
            grad_qkv.astype(jnp.bfloat16), "chan", scatter_dimension=0, tiled=True
        ).astype(jnp.float32),
        lax.psum_scatter(
            grad_out_proj.astype(jnp.bfloat16), "chan", scatter_dimension=0, tiled=True
        ).astype(jnp.float32),
        lax.psum_scatter(
            grad_one.astype(jnp.bfloat16), "chan", scatter_dimension=0, tiled=True
        ).astype(jnp.float32),
        lax.psum_scatter(
            grad_two.astype(jnp.bfloat16), "chan", scatter_dimension=0, tiled=True
        ).astype(jnp.float32),
    )
    weight_sums = lax.psum(
        (
            qkv_share,
            out_share,
            one_share,
            two_share,
            grad_conv_one,
            grad_conv_one_shift,
            grad_conv_two,
        ),
        "dp",
    )
    vector_sums = lax.psum(
        (
            grad_conv_two_shift,
            grad_lang,
            grad_gain_one,
            grad_shift_one,
            grad_q_shift,
            grad_v_shift,
            grad_out_shift,
            grad_gain_two,
            grad_shift_two,
            grad_one_shift,
            grad_two_shift,
        ),
        ("dp", "chan"),
    )
    return (
        encoded,
        mel_grad,
        weight_sums[4],
        weight_sums[5],
        weight_sums[6],
        vector_sums[0],
        vector_sums[1],
        vector_sums[2],
        vector_sums[3],
        weight_sums[0],
        vector_sums[4],
        vector_sums[5],
        weight_sums[1],
        vector_sums[6],
        vector_sums[7],
        vector_sums[8],
        weight_sums[2],
        vector_sums[9],
        weight_sums[3],
        vector_sums[10],
    )


def solution(mesh):
    in_specs = (
        P("dp", "chan", None),
        P("dp"),
        P(),
        P(None, "chan"),
        P("chan"),
        P(None, "chan", None),
        P(),
        P(),
        P(),
        P(),
        P("chan", None),
        P(),
        P(),
        P("chan", None),
        P(),
        P(),
        P(),
        P("chan", None),
        P(),
        P("chan", None),
        P(),
        P("dp", "chan", None),
    )
    out_specs = (
        P("dp", "chan", None),
        P("dp", "chan", None),
        P(None, "chan"),
        P("chan"),
        P(None, "chan", None),
        P(),
        P(),
        P(),
        P(),
        P("chan", None),
        P(),
        P(),
        P("chan", None),
        P(),
        P(),
        P(),
        P("chan", None),
        P(),
        P("chan", None),
        P(),
    )
    return jax.shard_map(
        on_device, mesh=mesh, in_specs=in_specs, out_specs=out_specs, check_vma=False
    )
```

profile of v0, /device:TPU:0, one launch (start us, length us, event | category | flops | bytes accessed | tf_op | source)
XLA Modules:
  0.0 1386.9 jit_solution(3937774967263430725)
XLA Ops:
  9.7 13.6 all_gather.24
  38.3 39.8 %slice.52 = bf16[2,1408,192]{1,2,0:T(8,128)(2,1)} slice(bf16[2,2817,192]{1,2,0:T(8,128)(2,1)S(1)} %pad.17), slice={[0:2:1], [2:2817:2], [0:192:1]} | slice | bytes 2162688 | tf_op jit(solution)/shard_map/slice | solution.py:50
  78.1 39.8 %slice.51 = bf16[2,1408,192]{1,2,0:T(8,128)(2,1)} slice(bf16[2,2817,192]{1,2,0:T(8,128)(2,1)S(1)} %pad.17), slice={[0:2:1], [1:2816:2], [0:192:1]} | slice | bytes 2162688 | tf_op jit(solution)/shard_map/slice | solution.py:49
  117.9 40.0 %slice.50 = bf16[2,1408,192]{1,2,0:T(8,128)(2,1)} slice(bf16[2,2817,192]{1,2,0:T(8,128)(2,1)S(1)} %pad.17), slice={[0:2:1], [0:2816:2], [0:192:1]} | slice | bytes 2162688 | tf_op jit(solution)/shard_map/slice | solution.py:48
  171.0 70.1 %reduce-scatter.9.cloned.1.call-done = f32[2,352,768]{2,1,0:T(8,128)} async-done(((f32[2,1408,768]{2,1,0:T(8,128)}), f32[2,352,768]{2,1,0:T(8,128)}) %reduce-scatter.9.cloned.1.call-update) | async-done | bytes 2162704 | tf_op jit(solution)/shard_map/reduce_scatter | solution.py:181
  251.4 22.1 %all-gather.8.cloned.1.call-done = bf16[768,2304]{1,0:T(8,128)(2,1)} async-done(((bf16[192,2304]{1,0:T(8,128)(2,1)}), bf16[768,2304]{1,0:T(8,128)(2,1)}) %all-gather.8.cloned.1.call-update) | async-done | bytes 3538960 | tf_op jit(solution)/shard_map/all_gather | solution.py:171
  291.7 23.9 %all-gather.12.cloned.1.call-done = bf16[2,1408,768]{2,1,0:T(8,128)(2,1)} async-done(((bf16[2,352,768]{2,1,0:T(8,128)(2,1)}), bf16[2,1408,768]{2,1,0:T(8,128)(2,1)}) %all-gather.12.cloned.1.call-update) | async-done | bytes 4325392 | tf_op jit(solution)/shard_map/all_gather | solution.py:210
  322.1 30.2 %all-gather.10.cloned.1.call-done = bf16[2,1408,768]{2,1,0:T(8,128)(2,1)} async-done(((bf16[2,352,768]{2,1,0:T(8,128)(2,1)}), bf16[2,1408,768]{2,1,0:T(8,128)(2,1)}) %all-gather.10.cloned.1.call-update) | async-done | bytes 4325392 | tf_op jit(solution)/shard_map/all_gather | solution.py:216
  358.8 75.2 %while.26 = (s32[]{:T(128)}, bf16[2,352,12,64]{1,3,2,0:T(8,128)(2,1)}, f32[2,12,352,1]{2,1,3,0:T(8,128)S(1)}, bf16[2,1408,12,64]{1,3,2,0:T(8,128)(2,1)}, bf16[2,...) while((s32[]{:T(128)}, bf16[2,352,12,64]{1,3,2,0:T(8,128)(2,1)}, ...), condition=%wide.region_6.7_spmd, body=%wide.region_3.6_spmd.sunk | while | flops 1570377600 | bytes 77041752 | solution.py:225
  358.8 13.1 multiply_reduce_fusion.10
  382.9 13.3 fusion.148
  396.1 13.1 multiply_reduce_fusion.10
  420.1 13.9 %fusion.148 = bf16[2,352,12,64]{1,3,2,0:T(8,128)(2,1)} fusion(bf16[2,352,12,64]{1,3,2,0:T(8,128)(2,1)} %get-tuple-element.376, s32[]{:T(128)S(6)} %copy.115, f32[12,352,1408]{2,1,0:T(8,128)} %get-tuple-element.353, f32[12,352]{1,0:T(8,128)S(1)} %get-tuple-element.355, bf16[2,1408,12,64]{1,3,2,0:T(8,128)(2,1)} %get-tuple-element.385), kind=kOutput, calls=%fused_computation.11.clone.1 | convolution fusion | flops 779378688 | bytes 26560000 | tf_op jit(solution)/shard_map/while/body/eval_jaxpr/hqk,khd->qhd/dot_general | solution.py:104
  456.4 27.4 %convert_reduce_fusion = (f32[3072]{0:T(1024)}, bf16[704,3072]{1,0:T(8,128)(2,1)S(1)}, f32[704,3072]{1,0:T(8,128)}) fusion(f32[704,3072]{1,0:T(8,128)} %fusion.93, f32[3072]{0:T(1024)S(1)} %copy-done.31, bf16[704,768]{1,0:T(8,128)(2,1)} %bitcast_convert_fusion, bf16[3072,768]{1,0:T(8,128)(2,1)} %all-gather.18.cloned.1.call-done), kind=kOutput, calls=%fused_computation.53 | convolution fusion | flops 3484087296 | bytes 27451392 | tf_op jit(solution)/shard_map/dot_general | solution.py:84
  496.1 132.5 %while.27 = (s32[]{:T(128)}, bf16[2,352,12,64]{1,3,2,0:T(8,128)(2,1)}, bf16[2,1408,12,64]{1,3,2,0:T(8,128)(2,1)}, bf16[2,1408,12,64]{1,3,2,0:T(8,128)(2,1)}, bf1...) while((s32[]{:T(128)}, ...), condition=%wide.region_13.14_spmd, body=%wide.region_11.13_spmd.sunk | while | flops 3855257600 | bytes 197090944 | solution.py:266
  509.6 15.9 %multiply_reduce_fusion.11 = (f32[12,352]{1,0:T(8,128)S(1)}, f32[12,352,1408]{2,1,0:T(8,128)}) fusion(f32[12,352,1408]{2,1,0:T(8,128)} %fusion.157, f32[12,352]{1,0:T(8,128)S(1)} %dynamic-slice_bitcast_fusion.2, bf16[2,1408,12,64]{1,3,2,0:T(8,128)(2,1)} %get-tuple-element.413, s32[]{:T(128)S(6)} %copy.125, ...), kind=kOutput, calls=%fused_computation.20.clone.1 | convolution fusion | flops 785051520 | bytes 50366464 | tf_op jit(solution)/shard_map/while/body/eval_jaxpr/qhd,khd->hqk/dot_general | solution.py:112
  525.5 15.3 %multiply_convert_fusion.5 = bf16[12,352,1408]{2,1,0:T(8,128)(2,1)S(1)} fusion(f32[12,352,1408]{2,1,0:T(8,128)} %get-tuple-element.366, f32[12,352,1408]{2,1,0:T(8,128)} %fusion.157, f32[12,352]{1,0:T(8,128)S(1)} %get-tuple-element.367), kind=kLoop, calls=%fused_computation.19.clone.1 | loop fusion | flops 17842176 | bytes 59490816 | tf_op jit(solution)/shard_map/while/body/eval_jaxpr/convert_element_type | solution.py:120
  575.7 15.9 %multiply_reduce_fusion.11 = (f32[12,352]{1,0:T(8,128)S(1)}, f32[12,352,1408]{2,1,0:T(8,128)}) fusion(f32[12,352,1408]{2,1,0:T(8,128)} %fusion.157, f32[12,352]{1,0:T(8,128)S(1)} %dynamic-slice_bitcast_fusion.2, bf16[2,1408,12,64]{1,3,2,0:T(8,128)(2,1)} %get-tuple-element.413, s32[]{:T(128)S(6)} %copy.125, ...), kind=kOutput, calls=%fused_computation.20.clone.1 | convolution fusion | flops 785051520 | bytes 50366464 | tf_op jit(solution)/shard_map/while/body/eval_jaxpr/qhd,khd->hqk/dot_general | solution.py:112
  591.6 15.3 %multiply_convert_fusion.5 = bf16[12,352,1408]{2,1,0:T(8,128)(2,1)S(1)} fusion(f32[12,352,1408]{2,1,0:T(8,128)} %get-tuple-element.366, f32[12,352,1408]{2,1,0:T(8,128)} %fusion.157, f32[12,352]{1,0:T(8,128)S(1)} %get-tuple-element.367), kind=kLoop, calls=%fused_computation.19.clone.1 | loop fusion | flops 17842176 | bytes 59490816 | tf_op jit(solution)/shard_map/while/body/eval_jaxpr/convert_element_type | solution.py:120
  658.6 152.8 %all-reduce.19.cloned.1.call-done = (bf16[2,1408,768]{2,0,1:T(2,128)(2,1)}, bf16[2,1408,768]{2,0,1:T(2,128)(2,1)}) async-done(((bf16[2,1408,768]{2,0,1:T(2,128)(2,1)}, bf16[2,1408,768]{2,0,1:T(2,128)(2,1)}), (bf16[2,1408,768]{2,0,1:T(2,128)(2,1)}, bf16[2,1408,768]{2,0,1:T(2,128)(2,1)})) %all-reduce.19.cloned.1.call-update) | async-done | bytes 8650768
  954.1 50.3 %reduce-scatter.17.cloned.1.call-done = bf16[768,768]{1,0:T(8,128)(2,1)} async-done(((bf16[3072,768]{1,0:T(8,128)(2,1)}), bf16[768,768]{1,0:T(8,128)(2,1)}) %reduce-scatter.17.cloned.1.call-update) | async-done | bytes 1179664 | tf_op jit(solution)/shard_map/reduce_scatter | solution.py:330
  1004.4 43.2 %reduce-scatter.11.cloned.1.call-done = bf16[192,2304]{1,0:T(8,128)(2,1)} async-done(((bf16[768,2304]{1,0:T(8,128)(2,1)}), bf16[192,2304]{1,0:T(8,128)(2,1)}) %reduce-scatter.11.cloned.1.call-update) | async-done | bytes 884752 | tf_op jit(solution)/shard_map/reduce_scatter | solution.py:321
  1047.6 296.0 %all-reduce.20 = (f32[192]{0:T(256)}, f32[192,2304]{1,0:T(8,128)}, f32[192,768]{1,0:T(8,128)}, f32[192,3072]{1,0:T(8,128)}, f32[768,768]{1,0:T(8,128)}) all-reduce(f32[192]{0:T(256)S(1)} %get-tuple-element.232, bf16[192,2304]{1,0:T(8,128)(2,1)} %reduce-scatter.11.cloned.1.call-done, ...), channel_id=1, replica_groups=mesh['dp'=8,'chan'=4] {'dp'}, use_global_device_ids=true, to_apply=%region_21.22 | all-reduce | flops 1769664 | bytes 10618368 | tf_op jit(solution)/shard_map/psum | solution.py:334
  1346.5 22.3 %all-reduce.17.cloned.1.call-done = (f32[240,192]{0,1:T(8,128)}, f32[3,192,768]{2,1,0:T(8,128)}) async-done(((f32[240,192]{0,1:T(8,128)}, f32[3,192,768]{2,1,0:T(8,128)}), (f32[240,192]{0,1:T(8,128)}, f32[3,192,768]{2,1,0:T(8,128)})) %all-reduce.17.cloned.1.call-update) | async-done | bytes 1953808 | tf_op jit(solution)/shard_map/psum | solution.py:334
  (344 shorter events, 382.9 us)
Async XLA Ops:
  7.2 150.7 %copy-start = (bf16[3,192,768]{2,1,0:T(8,128)(2,1)S(1)}, bf16[3,192,768]{2,1,0:T(8,128)(2,1)}, u32[]{:S(2)}) copy-start(bf16[3,192,768]{2,1,0:T(8,128)(2,1)} %param.31) | copy-start | bytes 2654212
  7.2 233.9 %reduce-scatter.9.cloned.1.call-start = ((), (), s32[]{:S(2)}) async-start(), calls=%async_computation.6 | async-start | bytes 10813440 | tf_op jit(solution)/shard_map/reduce_scatter | solution.py:181
  166.8 106.7 %all-gather.8.cloned.1.call-start = ((), (), s32[]{:S(2)}) async-start(), calls=%async_computation.7 | async-start | bytes 4423680 | tf_op jit(solution)/shard_map/all_gather | solution.py:171
  167.6 148.0 %all-gather.12.cloned.1.call-start = ((), (), s32[]{:S(2)}) async-start(), calls=%async_computation.9 | async-start | bytes 5406720 | tf_op jit(solution)/shard_map/all_gather | solution.py:210
  167.6 81.6 %copy-start.40 = (f32[768]{0:T(1024)}, f32[768]{0:T(1024)S(1)}, u32[]{:S(2)}) copy-start(f32[768]{0:T(1024)S(1)} %convert_element_type.185) | copy-start | bytes 9220
  167.7 81.0 %copy-start.38 = (f32[768]{0:T(1024)}, f32[768]{0:T(1024)S(1)}, u32[]{:S(2)}) copy-start(f32[768]{0:T(1024)S(1)} %convert_element_type.183) | copy-start | bytes 9220
  280.2 72.1 %all-gather.10.cloned.1.call-start = ((), (), s32[]{:S(2)}) async-start(), calls=%async_computation.8 | async-start | bytes 5406720 | tf_op jit(solution)/shard_map/all_gather | solution.py:216
  280.8 160.9 %all-gather.14.cloned.1.call-start = ((), (), s32[]{:S(2)}) async-start(), calls=%async_computation.10 | async-start | bytes 1474560 | tf_op jit(solution)/shard_map/all_gather | solution.py:172
  281.4 165.0 %all-gather.16.cloned.1.call-start = ((), (), s32[]{:S(2)}) async-start(), calls=%async_computation.11 | async-start | bytes 5898240 | tf_op jit(solution)/shard_map/all_gather | solution.py:173
  281.9 174.5 %all-gather.18.cloned.1.call-start = ((), (), s32[]{:S(2)}) async-start(), calls=%async_computation.12 | async-start | bytes 5898240 | tf_op jit(solution)/shard_map/all_gather | solution.py:174
  282.7 528.7 %all-reduce.19.cloned.1.call-start = ((), (), s32[]{:S(2)}) async-start(), calls=%async_computation.21 | async-start | bytes 17301504
  284.1 204.3 %copy-start.48 = (f32[768]{0:T(1024)}, f32[768]{0:T(1024)S(1)}, u32[]{:S(2)}) copy-start(f32[768]{0:T(1024)S(1)} %convert_element_type.192) | copy-start | bytes 9220
  284.1 162.3 %copy-start.54 = (f32[768]{0:T(1024)}, f32[768]{0:T(1024)S(1)}, u32[]{:S(2)}) copy-start(f32[768]{0:T(1024)S(1)} %convert_element_type.193) | copy-start | bytes 9220
  444.6 43.8 %copy-start.46 = (f32[704]{0:T(1024)}, f32[704]{0:T(1024)S(1)}, u32[]{:S(2)}) copy-start(f32[704]{0:T(1024)S(1)} %broadcast_multiply_fusion) | copy-start | bytes 8452
  446.3 42.0 %copy-start.50 = (f32[704]{0:T(1024)}, f32[704]{0:T(1024)S(1)}, u32[]{:S(2)}) copy-start(f32[704]{0:T(1024)S(1)} %fusion.83) | copy-start | bytes 8452
  653.7 224.3 %all-gather.20.cloned.1.call-start = ((), (), s32[]{:S(2)}) async-start(), calls=%async_computation.13 | async-start | bytes 5406720 | tf_op jit(solution)/shard_map/all_gather | solution.py:305
  839.3 107.2 %reduce-scatter.13.cloned.1.call-start = ((), (), s32[]{:S(2)}) async-start(), calls=%async_computation.15 | async-start | bytes 1474560 | tf_op jit(solution)/shard_map/reduce_scatter | solution.py:324
  843.2 110.9 %reduce-scatter.15.cloned.1.call-start = ((), (), s32[]{:S(2)}) async-start(), calls=%async_computation.16 | async-start | bytes 5898240 | tf_op jit(solution)/shard_map/reduce_scatter | solution.py:327
  851.5 152.9 %reduce-scatter.17.cloned.1.call-start = ((), (), s32[]{:S(2)}) async-start(), calls=%async_computation.17 | async-start | bytes 5898240 | tf_op jit(solution)/shard_map/reduce_scatter | solution.py:330
  870.5 177.1 %reduce-scatter.11.cloned.1.call-start = ((), (), s32[]{:S(2)}) async-start(), calls=%async_computation.14 | async-start | bytes 4423680 | tf_op jit(solution)/shard_map/reduce_scatter | solution.py:321
  877.7 465.8 %reduce-scatter.19.cloned.1.call-start = ((), (), s32[]{:S(2)}) async-start(), calls=%async_computation.18 | async-start | bytes 1802240
  922.4 424.1 %all-reduce.15.cloned.1.call-start = ((), (), s32[]{:S(2)}) async-start(), calls=%async_computation.19 | async-start | bytes 196608 | tf_op jit(solution)/shard_map/psum | solution.py:346
  929.2 439.6 %all-reduce.17.cloned.1.call-start = ((), (), s32[]{:S(2)}) async-start(), calls=%async_computation.20 | async-start | bytes 3932160 | tf_op jit(solution)/shard_map/psum | solution.py:334
  1346.5 32.7 %copy-start.56 = (f32[768]{0:T(1024)S(1)}, f32[768]{0:T(1024)}, u32[]{:S(2)}) copy-start(f32[768]{0:T(1024)} %get-tuple-element.438) | copy-start | bytes 9220
  (76 other events, 633.6 us)
Sparse Core Ops, SparseCore 0:
  166.9 74.1 reduce-scatter.8
  242.7 30.7 all-gather.7
  280.3 35.2 all-gather.11
  317.0 35.2 all-gather.9
  353.7 17.4 all-gather.13
  372.6 37.4 all-gather.15
  411.6 37.4 all-gather.17
  653.8 157.5 all-reduce.18
  839.4 35.3 all-gather.19
  877.8 25.7 reduce-scatter.12
  906.2 47.8 reduce-scatter.14
  956.5 47.8 reduce-scatter.16
  1007.1 40.4 reduce-scatter.10
  1050.0 27.3 reduce-scatter.18
  1086.5 138.5 all-reduce.14
  1229.3 139.5 all-reduce.16
where the time goes:
time: 1400 us; the launch traced here: 1390 us
  waiting for transfers between devices  426 us (30%)
  blocking collectives  310 us (22%)
  matrix products  283 us (20%)
  local copies, waits for them, and re-layouts  244 us (17%)
  other arithmetic  107 us (8%)
  between operations  16.3 us (1%)
    psum x1, blocking collectives, on_device(): lax.psum((qkv_share, out_share, one_share, two_share, grad_conv_one, grad...  296 us
    unnamed x18, waiting for transfers between devices  156 us
    reduce_scatter x1, waiting for transfers between devices, on_device(): lax.psum_scatter(dot_rows(hid_taps, conv_two.reshape(-1, model_width)), '...  70.1 us
    reduce_scatter x1, waiting for transfers between devices, on_device(): lax.psum_scatter(grad_two.astype(jnp.bfloat16), 'chan', scatter_dimension...  50.3 us
    dot_general x6, matrix products, dot_trans(): lax.dot_general(left, right, (((left.ndim - 1,), (1,)), ((), ())), prefer...  45.9 us
    reduce_scatter x1, waiting for transfers between devices, on_device(): lax.psum_scatter(grad_qkv.astype(jnp.bfloat16), 'chan', scatter_dimension...  43.2 us
    slice x1, local copies, waits for them, and re-layouts, taps_two(): frames[:, 0:2 * length:2]  40 us
    slice x1, local copies, waits for them, and re-layouts, taps_two(): frames[:, 2:2 * length + 1:2]  39.8 us
  transfers between devices with their start and end apart: 16, of which 9 were waited for; matrix products, arithmetic and copies ran while one was open for 17% of the time, Pallas kernels for 0%

commit v1 on v0

v1 whole, which is shorter than its diff:
```python
import math

import jax
import jax.numpy as jnp
from jax import lax
from jax.experimental import pallas as pl
from jax.experimental.pallas import tpu as pltpu
from jax.sharding import PartitionSpec as P

HEAD_DIM = 64
PAIR = 2 * HEAD_DIM
SCALE = HEAD_DIM ** (-0.5)
BF16 = jnp.bfloat16
F32 = jnp.float32

CORE = [(j, j ^ 1) for j in range(4)]
CROSS = [(j, j ^ 2) for j in range(4)]
SAME = [(2 * x + c, 2 * c + x) for x in range(2) for c in range(2)]
OTHER = [(2 * x + c, 2 * (1 - c) + x) for x in range(2) for c in range(2)]
SAME_BACK = [(b, a) for a, b in SAME]
OTHER_BACK = [(b, a) for a, b in OTHER]


def send(block, perm):
    return lax.ppermute(block, "chan", perm)


def ordered(first_is_own, own, other, axis=0, stack=False):
    join = jnp.stack if stack else jnp.concatenate
    return jnp.where(first_is_own, join([own, other], axis), join([other, own], axis))


def pick(block, index, axis):
    return lax.dynamic_index_in_dim(block, index, axis, keepdims=False)


def gelu_both(inputs):
    cdf = 0.5 * (1.0 + lax.erf(inputs * math.sqrt(0.5)))
    pdf = jnp.exp(-0.5 * inputs * inputs) * (1.0 / math.sqrt(2.0 * math.pi))
    return inputs * cdf, cdf + inputs * pdf


def norm_stats(inputs):
    row_mean = jnp.mean(inputs, axis=-1, keepdims=True)
    centered = inputs - row_mean
    variance = jnp.mean(centered * centered, axis=-1, keepdims=True)
    return row_mean, lax.rsqrt(variance + 1e-05)


def norm_back(inputs, stats, gain_vec, cotangent):
    row_mean, inverse = stats
    unit = (inputs - row_mean) * inverse
    scaled = cotangent * gain_vec
    mean_one = jnp.mean(scaled, axis=-1, keepdims=True)
    mean_two = jnp.mean(scaled * unit, axis=-1, keepdims=True)
    grad = inverse * (scaled - mean_one - unit * mean_two)
    return grad, jnp.sum(cotangent * unit, axis=0), jnp.sum(cotangent, axis=0)


def positions(frame_count, model_width, first_frame):
    increment = math.log(10000.0) / (model_width // 2 - 1)
    inverse = jnp.exp(-increment * jnp.arange(model_width // 2, dtype=jnp.float32))
    angles = (first_frame + jnp.arange(frame_count)).astype(jnp.float32)[:, None] * inverse[None, :]
    return jnp.concatenate([jnp.sin(angles), jnp.cos(angles)], axis=1)


def mm(left, right):
    return jnp.dot(left, right, preferred_element_type=F32)


def mm_nt(left, right):
    return lax.dot_general(left, right, (((1,), (1,)), ((), ())), preferred_element_type=F32)


def mm_tn(left, right):
    return lax.dot_general(left, right, (((0,), (0,)), ((), ())), preferred_element_type=F32)


def head_stack(block):
    lane = lax.broadcasted_iota(jnp.int32, block.shape, 1)
    zero = jnp.zeros_like(block)
    return jnp.concatenate(
        [jnp.where(lane < HEAD_DIM, block, zero), jnp.where(lane < HEAD_DIM, zero, block)], axis=0
    )


def head_join(stacked):
    rows = stacked.shape[0] // 2
    lane = lax.broadcasted_iota(jnp.int32, (rows, stacked.shape[1]), 1)
    return jnp.where(lane < HEAD_DIM, stacked[:rows], stacked[rows:])


def attend_kernel(chunk, q_ref, k_own, k_oth, v_own, v_oth, att_ref, lse_ref, k_all, v_all):
    rows = q_ref.shape[0]
    k_all[0:rows] = k_own[...]
    k_all[rows:] = k_oth[...]
    v_all[0:rows] = v_own[...]
    v_all[rows:] = v_oth[...]

    @pl.loop(0, rows // chunk)
    def _(step):
        at = pl.ds(pl.multiple_of(step * chunk, chunk), chunk)
        queries = head_stack(q_ref[at] * SCALE)
        scores = mm_nt(queries, k_all[...])
        top = jnp.max(scores, axis=1, keepdims=True)
        weights = jnp.exp(scores - top)
        total = jnp.sum(weights, axis=1, keepdims=True)
        out = mm(weights.astype(BF16), v_all[...]) / total
        att_ref[at] = head_join(out).astype(BF16)
        lse_ref[at] = head_join(jnp.broadcast_to(top + jnp.log(total), out.shape))


def attend(q, kv_own, kv_oth, heads):
    rows = q.shape[0]
    pairs = heads // 2
    chunk = 176
    spec = lambda shift: pl.BlockSpec((rows, PAIR), lambda p: (0, p + shift))
    return pl.pallas_call(
        lambda *refs: attend_kernel(chunk, *refs),
        grid=(pairs,),
        in_specs=[spec(0), spec(0), spec(0), spec(pairs), spec(pairs)],
        out_specs=[spec(0), spec(0)],
        out_shape=[
            jax.ShapeDtypeStruct((rows, pairs * PAIR), BF16),
            jax.ShapeDtypeStruct((rows, pairs * PAIR), F32),
        ],
        scratch_shapes=[pltpu.VMEM((2 * rows, PAIR), BF16)] * 2,
        compiler_params=pltpu.CompilerParams(vmem_limit_bytes=48 * 1024 * 1024),
        cost_estimate=pl.CostEstimate(
            flops=pairs * 16 * rows * rows * PAIR,
            bytes_accessed=pairs * PAIR * rows * 16,
            transcendentals=4 * pairs * rows * rows,
        ),
        name="attend",
    )(q, kv_own, kv_oth, kv_own, kv_oth)


def attend_back_kernel(
    chunk,
    q_ref, k_own, k_oth, v_own, v_oth, lse_ref, g_ref,
    dq_ref, dk_own, dk_oth, dv_own, dv_oth,
    k_all, v_all, q_all, g_all, p_all, s_all,
):
    rows = q_ref.shape[0]
    k_all[0:rows] = k_own[...]
    k_all[rows:] = k_oth[...]
    v_all[0:rows] = v_own[...]
    v_all[rows:] = v_oth[...]

    @pl.loop(0, rows // chunk)
    def _(step):
        at = pl.ds(pl.multiple_of(step * chunk, chunk), chunk)
        both = pl.ds(pl.multiple_of(2 * step * chunk, 2 * chunk), 2 * chunk)
        queries = head_stack(q_ref[at] * SCALE)
        grads = head_stack(g_ref[at])
        q_all[both] = queries
        g_all[both] = grads
        lse = jnp.concatenate([lse_ref[at, 0:1], lse_ref[at, HEAD_DIM : HEAD_DIM + 1]], axis=0)
        probs = jnp.exp(mm_nt(queries, k_all[...]) - lse)
        grad_probs = mm_nt(grads, v_all[...])
        inner = jnp.sum(probs * grad_probs, axis=1, keepdims=True)
        grad_scores = (probs * (grad_probs - inner)).astype(BF16)
        p_all[both] = probs.astype(BF16)
        s_all[both] = grad_scores
        dq_ref[at] = (head_join(mm(grad_scores, k_all[...])) * SCALE).astype(BF16)

    dv = mm_tn(g_all[...], p_all[...]).T.astype(BF16)
    dv_own[...] = dv[0:rows]
    dv_oth[...] = dv[rows:]
    dk = mm_tn(q_all[...], s_all[...]).T.astype(BF16)
    dk_own[...] = dk[0:rows]
    dk_oth[...] = dk[rows:]


def attend_back(q, kv_own, kv_oth, lse, grad_att, heads):
    rows = q.shape[0]
    pairs = heads // 2
    chunk = 176
    spec = lambda shift: pl.BlockSpec((rows, PAIR), lambda p: (0, p + shift))
    shape = jax.ShapeDtypeStruct((rows, pairs * PAIR), BF16)
    return pl.pallas_call(
        lambda *refs: attend_back_kernel(chunk, *refs),
        grid=(pairs,),
        in_specs=[spec(0), spec(0), spec(0), spec(pairs), spec(pairs), spec(0), spec(0)],
        out_specs=[spec(0)] * 5,
        out_shape=[shape] * 5,
        scratch_shapes=[pltpu.VMEM((2 * rows, PAIR), BF16)] * 4
        + [pltpu.VMEM((2 * rows, 2 * rows), BF16)] * 2,
        compiler_params=pltpu.CompilerParams(vmem_limit_bytes=48 * 1024 * 1024),
        cost_estimate=pl.CostEstimate(
            flops=pairs * 40 * rows * rows * PAIR,
            bytes_accessed=pairs * PAIR * rows * 26,
            transcendentals=4 * pairs * rows * rows,
        ),
        name="attend_back",
    )(q, kv_own, kv_oth, kv_own, kv_oth, lse, grad_att)


def gather_rows(part, x, c, axis=0):
    across = send(part, CROSS)
    column = ordered(x == 0, part, across, axis, stack=True)
    beside = send(column, CORE)
    whole = ordered(c == 0, column, beside, axis + 1, stack=True)
    shape = list(part.shape)
    shape[axis] *= 4
    return whole.reshape(shape)


def round_sum(*terms):
    return sum(term.astype(F32) for term in terms).astype(BF16)


def share_rows(make, x, c):
    beside = send(make(1 - c).astype(BF16), CORE)
    column = (make(c) + beside.astype(F32)).astype(BF16)
    across = send(pick(column, 1 - x, 0), CROSS)
    return round_sum(pick(column, x, 0), across)


def sum_dp(share):
    count = lax.axis_size("dp")
    index = lax.axis_index("dp")
    bits = []
    step = 1
    while step < count:
        bits.append(step)
        step *= 2
    for bit in bits:
        side = (index // bit) % 2
        halves = share.reshape((2, share.shape[0] // 2) + share.shape[1:])
        perm = [(d, d ^ bit) for d in range(count)]
        arrived = lax.ppermute(pick(halves, 1 - side, 0), "dp", perm)
        share = round_sum(pick(halves, side, 0), arrived)
    for bit in reversed(bits):
        side = (index // bit) % 2
        perm = [(d, d ^ bit) for d in range(count)]
        arrived = lax.ppermute(share, "dp", perm)
        share = ordered(side == 0, share, arrived)
    return share


def on_device(
    mel,
    lang_group,
    clip_count,
    conv_one,
    conv_one_bias,
    conv_two,
    conv_two_bias,
    lang_table,
    ln_one_gain,
    ln_one_bias,
    w_qkv,
    q_bias,
    v_bias,
    w_out,
    out_bias,
    ln_two_gain,
    ln_two_bias,
    w_fc_one,
    fc_one_bias,
    w_fc_two,
    fc_two_bias,
    grad_out,
):
    slots, part, width = grad_out.shape
    heads = width // HEAD_DIM
    mels = mel.shape[2]
    rows = slots * part
    j = lax.axis_index("chan")
    x, c = j // 2, j % 2
    live = (x < clip_count[lax.axis_index("dp")]).astype(F32)

    def to_clip(block):
        same = send(pick(block, c, 0), SAME)
        other = send(pick(block, 1 - c, 0), OTHER)
        return ordered(x == 0, same, other)

    def from_clip(block):
        half = block.shape[0] // 2
        first, second = block[:half], block[half:]
        same = send(jnp.where(x == 0, first, second), SAME_BACK)
        other = send(jnp.where(x == 0, second, first), OTHER_BACK)
        return ordered(c == 0, same, other, stack=True)

    mel_pairs = mel.reshape(slots, part, 2 * mels)
    edge = send(jnp.where(j == 1, mel_pairs[1, -1], mel_pairs[0, 0]), [(1, 3), (2, 0)])
    edge = jnp.where(j == 1, mel_pairs[0, -1], jnp.where(j == 2, mel_pairs[1, 0], edge))
    zero_edge = jnp.zeros_like(edge)
    mel_own = jnp.concatenate(
        [
            jnp.where(c == 1, edge, zero_edge)[None],
            to_clip(mel_pairs),
            jnp.where(c == 0, edge, zero_edge)[None],
        ]
    )
    bias_full = gather_rows(conv_one_bias, x, c)
    one_full = gather_rows(conv_one, x, c, axis=1)
    two_full = gather_rows(conv_two, x, c, axis=1).reshape(-1, width)
    qkv_full = gather_rows(w_qkv, x, c)
    out_full = gather_rows(w_out, x, c)
    up_full = gather_rows(w_fc_one, x, c)
    down_full = gather_rows(w_fc_two, x, c)
    cotangent = to_clip(grad_out)

    even, odd = mel_own[:, :mels], mel_own[:, mels:]
    cols_even = jnp.concatenate(
        [odd[0:rows], even[1 : rows + 1], odd[1 : rows + 1]], axis=1
    )
    cols_odd = jnp.concatenate(
        [even[1 : rows + 1], odd[1 : rows + 1], even[2 : rows + 2]], axis=1
    )
    cols_edge = jnp.concatenate([even[0:1], odd[0:1], even[1:2]], axis=1)
    shift = bias_full.astype(F32)
    hid_even, slope_even = gelu_both(mm(cols_even, one_full) + shift)
    hid_odd, slope_odd = gelu_both(mm(cols_odd, one_full) + shift)
    hid_edge, _ = gelu_both(mm(cols_edge, one_full) + shift)
    hid_edge = jnp.where(c == 1, hid_edge, 0.0)
    hid_even, hid_odd, hid_edge = hid_even.astype(BF16), hid_odd.astype(BF16), hid_edge.astype(BF16)
    slope_even, slope_odd = slope_even.astype(BF16), slope_odd.astype(BF16)
    hid_prev = jnp.concatenate([hid_edge, hid_odd[:-1]])
    hid_taps = jnp.concatenate([hid_prev, hid_even, hid_odd], axis=1)
    stem_act, slope_two = gelu_both(mm(hid_taps, two_full) + conv_two_bias.astype(F32))
    slope_two = slope_two.astype(BF16)
    group = pick(lang_group, x, 0)
    stem = stem_act + positions(rows, width, c * rows) + pick(lang_table, group, 0).astype(F32)[None]

    gain_one, gain_two = ln_one_gain.astype(F32), ln_two_gain.astype(F32)
    stats_one = norm_stats(stem)
    normed = (
        (stem - stats_one[0]) * stats_one[1] * gain_one + ln_one_bias.astype(F32)
    ).astype(BF16)
    kv_shift = jnp.concatenate([jnp.zeros((width,), F32), v_bias.astype(F32)])
    kv_own = (mm(normed, qkv_full[:, width:]) + kv_shift).astype(BF16)
    kv_oth = send(kv_own, CORE)
    queries = (mm(normed, qkv_full[:, :width]) + q_bias.astype(F32)).astype(BF16)
    attended, lse = attend(queries, kv_own, kv_oth, heads)
    residual = stem + mm(attended, out_full) + out_bias.astype(F32)

    stats_two = norm_stats(residual)
    normed_two = (
        (residual - stats_two[0]) * stats_two[1] * gain_two + ln_two_bias.astype(F32)
    ).astype(BF16)
    active, slope_up = gelu_both(mm(normed_two, up_full) + fc_one_bias.astype(F32))
    active, slope_up = active.astype(BF16), slope_up.astype(BF16)
    encoded = (residual + mm(active, down_full) + fc_two_bias.astype(F32)) * live
    encoded = from_clip(encoded.astype(BF16))

    def weight_grad(left, right):
        split = left.reshape(left.shape[0], 2, 2, left.shape[1] // 4)

        def make(core):
            half = pick(split, core, 2).reshape(left.shape[0], -1)
            return mm_tn(half, right).reshape(2, -1, right.shape[1])

        return share_rows(make, x, c)

    grad_mlp = (cotangent.astype(F32) * live).astype(BF16)
    grad_rows = grad_mlp.astype(F32)
    down_share = weight_grad(active, grad_mlp)
    down_shift = jnp.sum(grad_rows, axis=0)
    grad_upper = (mm_nt(grad_mlp, down_full) * slope_up.astype(F32)).astype(BF16)
    up_share = weight_grad(normed_two, grad_upper)
    up_shift = jnp.sum(grad_upper.astype(F32), axis=0)
    grad_norm, grad_gain_two, grad_shift_two = norm_back(
        residual, stats_two, gain_two, mm_nt(grad_upper, up_full)
    )
    grad_residual = grad_rows + grad_norm
    grad_branch = grad_residual.astype(BF16)
    out_share = weight_grad(attended, grad_branch)
    out_shift = jnp.sum(grad_branch.astype(F32), axis=0)
    grad_att = mm_nt(grad_branch, out_full).astype(BF16)
    grad_q, dk_own, dk_oth, dv_own, dv_oth = attend_back(
        queries, kv_own, kv_oth, lse, grad_att, heads
    )
    grad_k = round_sum(dk_own, send(dk_oth, CORE))
    grad_v = round_sum(dv_own, send(dv_oth, CORE))
    grad_packed = jnp.concatenate([grad_q, grad_k, grad_v], axis=1)
    qkv_share = weight_grad(normed, grad_packed)
    q_shift = jnp.sum(grad_q.astype(F32), axis=0)
    v_shift = jnp.sum(grad_v.astype(F32), axis=0)
    grad_norm, grad_gain_one, grad_shift_one = norm_back(
        stem, stats_one, gain_one, mm_nt(grad_packed, qkv_full)
    )
    grad_stem = grad_residual + grad_norm
    group_hot = (jnp.arange(lang_table.shape[0]) == group).astype(F32)
    grad_lang = group_hot[:, None] * jnp.sum(grad_stem, axis=0)[None]
    grad_two = (grad_stem * slope_two.astype(F32)).astype(BF16)
    two_shift = jnp.sum(grad_two.astype(F32), axis=0)
    follow = send(grad_two[0:1], [(1, 0), (3, 2)])
    grad_next = jnp.concatenate([grad_two[1:], follow])

    taps = hid_taps.reshape(rows, 3, 2, 2, width // 4)

    def make_two(core):
        half = pick(taps, core, 3).reshape(rows, -1)
        grads = mm_tn(half, grad_two).reshape(3, 2, width // 4, width)
        return jnp.moveaxis(grads, 1, 0)

    two_share = share_rows(make_two, x, c).reshape(-1, width)
    hid_grad_even = mm_nt(grad_two, two_full[width : 2 * width])
    hid_grad_odd = mm_nt(grad_two, two_full[2 * width :]) + mm_nt(grad_next, two_full[:width])
    grad_even = (hid_grad_even * slope_even.astype(F32)).astype(BF16)
    grad_odd = (hid_grad_odd * slope_odd.astype(F32)).astype(BF16)
    one_shift = jnp.sum(grad_even.astype(F32), axis=0) + jnp.sum(grad_odd.astype(F32), axis=0)

    split_even = grad_even.reshape(rows, 2, 2, width // 4)
    split_odd = grad_odd.reshape(rows, 2, 2, width // 4)

    def make_one(core):
        half_even = pick(split_even, core, 2).reshape(rows, -1)
        half_odd = pick(split_odd, core, 2).reshape(rows, -1)
        grads = mm_tn(half_even, cols_even) + mm_tn(half_odd, cols_odd)
        return grads.reshape(2, width // 4, 3 * mels)

    one_share = share_rows(make_one, x, c)
    terms_even = mm_nt(grad_even, one_full)
    terms_odd = mm_nt(grad_odd, one_full)
    before, mid_e, after = terms_even[:, :mels], terms_even[:, mels : 2 * mels], terms_even[:, 2 * mels :]
    first_o, mid_o, last_o = terms_odd[:, :mels], terms_odd[:, mels : 2 * mels], terms_odd[:, 2 * mels :]
    spill = send(jnp.where(c == 0, last_o[-1:], before[0:1]), CORE)
    zero_spill = jnp.zeros_like(spill)
    last_prev = jnp.concatenate([jnp.where(c == 1, spill, zero_spill), last_o[:-1]])
    before_next = jnp.concatenate([before[1:], jnp.where(c == 0, spill, zero_spill)])
    mel_grad = jnp.concatenate([mid_e + first_o + last_prev, after + mid_o + before_next], axis=1)
    mel_grad = from_clip(mel_grad.astype(BF16)).astype(F32).reshape(slots, 2 * part, mels)

    down_sum = sum_dp(down_share)
    up_sum = sum_dp(up_share)
    out_sum = sum_dp(out_share)
    qkv_sum = sum_dp(qkv_share)
    two_sum = sum_dp(two_share)
    one_sum = sum_dp(one_share)
    early = lax.psum(
        jnp.concatenate([down_shift, up_shift, grad_gain_two, grad_shift_two, out_shift]),
        ("dp", "chan"),
    )
    late = lax.psum(
        jnp.concatenate(
            [
                q_shift, v_shift, grad_gain_one, grad_shift_one, two_shift, one_shift,
                grad_lang.reshape(-1),
            ]
        ),
        ("dp", "chan"),
    )
    up_end = width + up_shift.shape[0]
    vec = lambda packed, start: packed[start : start + width]
    return (
        encoded,
        mel_grad,
        one_sum.astype(F32).T,
        lax.dynamic_slice_in_dim(vec(late, 5 * width), j * (width // 4), width // 4),
        two_sum.astype(F32).reshape(conv_two.shape),
        vec(late, 4 * width),
        late[6 * width :].reshape(lang_table.shape),
        vec(late, 2 * width),
        vec(late, 3 * width),
        qkv_sum.astype(F32),
        vec(late, 0),
        vec(late, width),
        out_sum.astype(F32),
        vec(early, up_end + 2 * width),
        vec(early, up_end),
        vec(early, up_end + width),
        up_sum.astype(F32),
        early[width:up_end],
        down_sum.astype(F32),
        vec(early, 0),
    )


def solution(mesh):
    in_specs = (
        P("dp", "chan", None),
        P("dp"),
        P(),
        P(None, "chan"),
        P("chan"),
        P(None, "chan", None),
        P(),
        P(),
        P(),
        P(),
        P("chan", None),
        P(),
        P(),
        P("chan", None),
        P(),
        P(),
        P(),
        P("chan", None),
        P(),
        P("chan", None),
        P(),
        P("dp", "chan", None),
    )
    out_specs = (
        P("dp", "chan", None),
        P("dp", "chan", None),
        P(None, "chan"),
        P("chan"),
        P(None, "chan", None),
        P(),
        P(),
        P(),
        P(),
        P("chan", None),
        P(),
        P(),
        P("chan", None),
        P(),
        P(),
        P(),
        P("chan", None),
        P(),
        P("chan", None),
        P(),
    )
    return jax.shard_map(
        on_device, mesh=mesh, in_specs=in_specs, out_specs=out_specs, check_vma=False
    )
```

time: 1400 us -> 862 us (0.62)
  blocking collectives: 310 us -> 40.6 us
  matrix products: 283 us -> 102 us
  local copies, waits for them, and re-layouts: 244 us -> 93.7 us
  starting transfers between devices: 1.4 us -> 90.1 us
  Pallas kernels: 0 us -> 85.5 us
  waiting for transfers between devices: 426 us -> 347 us
  other arithmetic: 107 us -> 79.5 us
    psum x1, blocking collectives: 296 us -> 40.6 us  [on_device(): lax.psum(jnp.concatenate([down_shift, up_shift, grad_gain_two, grad_shift...]
    ppermute x0 -> x76, waiting for transfers between devices: none -> 253 us  [the longest x40 150 us: send(): return lax.ppermute(block, 'chan', perm)]
    dot_general x34 -> x32, matrix products: 283 us -> 102 us  [the longest x14 36.4 us: mm_tn(): lax.dot_general(left, right, (((0,), (0,)), ((), ())), preferred_element_...]
    reduce_scatter x5 -> x0, waiting for transfers between devices: 171 us -> none  [the longest x1 70.1 us: on_device(): lax.psum_scatter(dot_rows(hid_taps, conv_two.reshape(-1, model_width)), '...]
    unnamed x18 -> x1, waiting for transfers between devices: 156 us -> 0.02 us
    slice x7 -> x11, local copies, waits for them, and re-layouts: 123 us -> 11.1 us  [the longest x1 2.49 us: on_device(): grad_next = jnp.concatenate([grad_two[1:], follow])]
    ppermute x0 -> x76, starting transfers between devices: none -> 90.1 us  [the longest x40 45.7 us: send(): return lax.ppermute(block, 'chan', perm)]
    pallas_call x0 -> x2, Pallas kernels: none -> 85.5 us  [the longest x1 50.7 us: attend_back(): pl.pallas_call(lambda *refs: attend_back_kernel(chunk, *refs), grid=(pair...]
  transfers between devices with their start and end apart: 16 -> 77, of which waited for: 9 -> 39; matrix products, arithmetic and copies ran while one was open for 17% -> 24% of each run, Pallas kernels for 0% -> 10%
where the time goes in v1:
time: 862 us; the launch traced here: 857 us
  waiting for transfers between devices  347 us (40%)
  matrix products  102 us (12%)
  local copies, waits for them, and re-layouts  93.7 us (11%)
  starting transfers between devices  90.1 us (10%)
  Pallas kernels  85.5 us (10%)
  other arithmetic  79.5 us (9%)
  blocking collectives  40.6 us (5%)
  between operations  19 us (2%)
    ppermute x40, waiting for transfers between devices, send(): return lax.ppermute(block, 'chan', perm)  150 us
    psum x1, waiting for transfers between devices, on_device(): lax.psum(jnp.concatenate([q_shift, v_shift, grad_gain_one, grad_shift_one...  94.4 us
    ppermute x18, waiting for transfers between devices, sum_dp(): arrived = lax.ppermute(share, 'dp', perm)  58.3 us
    pallas_call x1, Pallas kernels, attend_back(): pl.pallas_call(lambda *refs: attend_back_kernel(chunk, *refs), grid=(pair...  50.7 us
    ppermute x40, starting transfers between devices, send(): return lax.ppermute(block, 'chan', perm)  45.7 us
    ppermute x18, waiting for transfers between devices, sum_dp(): arrived = lax.ppermute(pick(halves, 1 - side, 0), 'dp', perm)  44.6 us
    psum x1, blocking collectives, on_device(): lax.psum(jnp.concatenate([down_shift, up_shift, grad_gain_two, grad_shift...  40.6 us
    select_n x35, other arithmetic, ordered(): jnp.where(first_is_own, join([own, other], axis), join([other, own], axis))  36.6 us
  transfers between devices with their start and end apart: 77, of which 39 were waited for; matrix products, arithmetic and copies ran while one was open for 24% of the time, Pallas kernels for 10%

profile of v1, /device:TPU:0, one launch (start us, length us, event | category | flops | bytes accessed | tf_op | source)
XLA Modules:
  0.0 857.1 jit_solution(843851271285805242)
XLA Ops:
  41.0 5.8 collective-permute-start.20
  70.1 10.3 %collective-permute-done.9 = bf16[192,2304]{1,0:T(8,128)(2,1)} collective-permute-done((bf16[192,2304]{1,0:T(8,128)(2,1)}, bf16[192,2304]{1,0:T(8,128)(2,1)}, u32[]{:S(2)}, u32[]{:S(2)}) %collective-permute-start.9) | collective-permute-done | bytes 884768 | tf_op jit(solution)/shard_map/ppermute | solution.py:25
  86.5 30.7 %collective-permute-done.14 = bf16[192,3072]{1,0:T(8,128)(2,1)S(1)} collective-permute-done((bf16[192,3072]{1,0:T(8,128)(2,1)}, bf16[192,3072]{1,0:T(8,128)(2,1)S(1)}, u32[]{:S(2)}, u32[]{:S(2)}) %collective-permute-start.14) | collective-permute-done | bytes 1179680 | tf_op jit(solution)/shard_map/ppermute | solution.py:25
  118.9 23.0 %collective-permute-done.16 = bf16[768,768]{1,0:T(8,128)(2,1)S(1)} collective-permute-done((bf16[768,768]{1,0:T(8,128)(2,1)S(1)}, bf16[768,768]{1,0:T(8,128)(2,1)S(1)}, u32[]{:S(2)}, u32[]{:S(2)}) %collective-permute-start.16) | collective-permute-done | bytes 1179680 | tf_op jit(solution)/shard_map/ppermute | solution.py:25
  168.5 6.3 maximum_select_fusion
  180.5 34.8 %attend.1 = (bf16[704,768]{1,0:T(8,128)(2,1)S(1)}, f32[704,768]{1,0:T(8,128)S(1)}) custom-call(bf16[704,768]{1,0:T(8,128)(2,1)S(1)} %add_convert_fusion.7.refs_0_, bf16[704,1536]{1,0:T(8,128)(2,1)} %add_convert_fusion.2.refs_1_.refs_3_, bf16[704,1536]{1,0:T(8,128)(2,1)} %collective-permute-done.11.refs_2_.refs_4_, ...), custom_call_target="tpu_custom_call" | custom-call | flops 6090129408 | bytes 8650752 | tf_op jit(solution)/shard_map/attend/pallas_call | solution.py:118
  223.8 8.4 multiply_convert_fusion.1
  232.2 7.9 reshape.860
  240.1 8.3 multiply_convert_fusion.6
  248.4 9.9 %convert_reduce_fusion = (f32[3072]{0:T(1024)S(1)}, bf16[704,3072]{1,0:T(8,128)(2,1)S(1)}) fusion(f32[704,3072]{1,0:T(8,128)} %get-tuple-element.143, f32[3072]{0:T(1024)S(1)} %copy-done.61, bf16[3072,768]{1,0:T(8,128)(2,1)} %bitcast.393, bf16[352,768]{1,0:T(8,128)(2,1)} %collective-permute-done.21, bf16[352,768]{1,0:T(8,128)(2,1)} %collective-permute-done.20, ...), kind=kOutput, calls=%fused_computation.6 | convolution fusion | flops 3360814080 | bytes 18800644 | tf_op jit(solution)/shard_map/dot_general | solution.py:72
  265.6 31.1 %dynamic-slice_reduce_fusion.1 = (bf16[704,2,768]{2,1,0:T(2,128)(2,1)}, bf16[704,2,768]{2,1,0:T(2,128)(2,1)}) fusion(bf16[704,2,2,768]{3,2,1,0:T(2,128)(2,1)S(1)} %bitcast.370, s32[]{:T(128)S(6)} %select_n.758, s32[]{:T(128)S(6)} %select_n.759), kind=kLoop, calls=%fused_computation.19 | loop fusion | bytes 8650760 | tf_op jit(solution)/shard_map/jit(dynamic_index_in_dim)/dynamic_slice | solution.py:34
  314.5 50.7 %attend_back.1 = (bf16[704,768]{1,0:T(8,128)(2,1)S(1)}, bf16[704,768]{1,0:T(8,128)(2,1)S(1)}, bf16[704,768]{1,0:T(8,128)(2,1)}, bf16[704,768]{1,0:T(8,128)(2,1)S(1)}, bf16[704,768]{1,0:T(8,128)(2,1)S(1)}) custom-call(bf16[704,768]{1,0:T(8,128)(2,1)} %copy-done.2, bf16[704,1536]{1,0:T(8,128)(2,1)} %add_convert_fusion.2.refs_1_.refs_3_, ...), custom_call_target="tpu_custom_call" | custom-call | flops 15225323520 | bytes 14057472 | tf_op jit(solution)/shard_map/attend_back/pallas_call | solution.py:181
  368.7 40.6 %psum.15 = f32[6144]{0:T(1024)S(1)} all-reduce(f32[6144]{0:T(1024)S(1)} %constant_dynamic-update-slice_fusion.11), channel_id=1, replica_groups=mesh['dp'=8,'chan'=4] {'dp','chan'}, use_global_device_ids=true, to_apply=%region_22.23 | all-reduce | flops 6144 | bytes 49152 | tf_op jit(solution)/shard_map/psum | solution.py:434
  496.5 7.1 collective-permute-done.29
  504.0 94.4 %all-reduce.3.cloned.1.call-done = f32[16896]{0:T(1024)} async-done(((f32[16896]{0:T(1024)}), f32[16896]{0:T(1024)}) %all-reduce.3.cloned.1.call-update) | async-done | bytes 67600 | tf_op jit(solution)/shard_map/psum | solution.py:438
  656.6 12.9 %collective-permute-done.61 = bf16[192,3072]{1,0:T(8,128)(2,1)S(1)} collective-permute-done((bf16[192,3072]{1,0:T(8,128)(2,1)S(1)}, bf16[192,3072]{1,0:T(8,128)(2,1)S(1)}, u32[]{:S(2)}, u32[]{:S(2)}) %collective-permute-start.61) | collective-permute-done | bytes 1179680 | tf_op jit(solution)/shard_map/ppermute | solution.py:25
  671.7 23.1 %collective-permute-done.69 = bf16[768,768]{1,0:T(8,128)(2,1)S(1)} collective-permute-done((bf16[768,768]{1,0:T(8,128)(2,1)S(1)}, bf16[768,768]{1,0:T(8,128)(2,1)S(1)}, u32[]{:S(2)}, u32[]{:S(2)}) %collective-permute-start.69) | collective-permute-done | bytes 1179680 | tf_op jit(solution)/shard_map/ppermute | solution.py:25
  696.8 16.9 %collective-permute-done.45 = bf16[192,2304]{1,0:T(8,128)(2,1)S(1)} collective-permute-done((bf16[192,2304]{1,0:T(8,128)(2,1)S(1)}, bf16[192,2304]{1,0:T(8,128)(2,1)S(1)}, u32[]{:S(2)}, u32[]{:S(2)}) %collective-permute-start.45) | collective-permute-done | bytes 884768 | tf_op jit(solution)/shard_map/ppermute | solution.py:25
  715.7 15.7 %collective-permute-done.37 = bf16[3,192,768]{2,1,0:T(8,128)(2,1)S(1)} collective-permute-done((bf16[3,192,768]{2,1,0:T(8,128)(2,1)S(1)}, bf16[3,192,768]{2,1,0:T(8,128)(2,1)S(1)}, u32[]{:S(2)}, u32[]{:S(2)}) %collective-permute-start.37) | collective-permute-done | bytes 884768 | tf_op jit(solution)/shard_map/ppermute | solution.py:25
  744.9 10.9 %collective-permute-done.47 = bf16[48,2304]{1,0:T(8,128)(2,1)S(1)} collective-permute-done((bf16[48,2304]{1,0:T(8,128)(2,1)S(1)}, bf16[48,2304]{1,0:T(8,128)(2,1)S(1)}, u32[]{:S(2)}, u32[]{:S(2)}) %collective-permute-start.47) | collective-permute-done | bytes 221216 | tf_op jit(solution)/shard_map/ppermute | solution.py:232
  763.0 10.0 %collective-permute-done.48 = bf16[24,2304]{1,0:T(8,128)(2,1)S(1)} collective-permute-done((bf16[24,2304]{1,0:T(8,128)(2,1)S(1)}, bf16[24,2304]{1,0:T(8,128)(2,1)S(1)}, u32[]{:S(2)}, u32[]{:S(2)}) %collective-permute-start.48) | collective-permute-done | bytes 110624 | tf_op jit(solution)/shard_map/ppermute | solution.py:232
  776.1 7.5 collective-permute-done.64
  786.9 6.9 collective-permute-done.49
  830.5 10.9 %collective-permute-done.67 = bf16[96,3072]{1,0:T(8,128)(2,1)S(1)} collective-permute-done((bf16[96,3072]{1,0:T(8,128)(2,1)S(1)}, bf16[96,3072]{1,0:T(8,128)(2,1)S(1)}, u32[]{:S(2)}, u32[]{:S(2)}) %collective-permute-start.67) | collective-permute-done | bytes 589856 | tf_op jit(solution)/shard_map/ppermute | solution.py:237
  (544 shorter events, 353.9 us)
Async XLA Ops:
  7.3 591.1 %all-reduce.3.cloned.1.call-start = ((), (), s32[]{:S(2)}) async-start(), calls=%async_computation | async-start | bytes 139264 | tf_op jit(solution)/shard_map/psum | solution.py:438
  10.5 40.0 %collective-permute-start.12 = (bf16[192,768]{1,0:T(8,128)(2,1)}, bf16[192,768]{1,0:T(8,128)(2,1)S(1)}, u32[]{:S(2)}, u32[]{:S(2)}) collective-permute-start(bf16[192,768]{1,0:T(8,128)(2,1)} %param.35), channel_id=1, source_target_pairs={{0,2},{1,3},{2,0},{3,1},{4,6},{5,7},{6,4},{7,5},{8,10},{9,11},{10,... | collective-permute-start | bytes 884744 | tf_op jit(solution)/shard_map/ppermute | solution.py:25
  40.4 40.0 %collective-permute-start.9 = (bf16[192,2304]{1,0:T(8,128)(2,1)}, bf16[192,2304]{1,0:T(8,128)(2,1)}, u32[]{:S(2)}, u32[]{:S(2)}) collective-permute-start(bf16[192,2304]{1,0:T(8,128)(2,1)} %param.32), channel_id=1, source_target_pairs={{0,2},{1,3},{2,0},{3,1},{4,6},{5,7},{6,4},{7,5},{8,10},{9,11},{10,... | collective-permute-start | bytes 2654216 | tf_op jit(solution)/shard_map/ppermute | solution.py:25
  41.0 207.4 %collective-permute-start.20 = (bf16[352,768]{1,0:T(8,128)(2,1)}, bf16[352,768]{1,0:T(8,128)(2,1)}, u32[]{:S(2)}, u32[]{:S(2)}) collective-permute-start(bf16[352,768]{1,0:T(8,128)(2,1)} %get-tuple-element.114), channel_id=1, source_target_pairs={{0,0},{1,2},{2,1},{3,3},{4,4},{5,6},{6,5},{7,7},{8,8},{9,10},{10,9... | collective-permute-start | bytes 1622024 | tf_op jit(solution)/shard_map/ppermute | solution.py:25
  46.9 201.5 %collective-permute-start.21 = (bf16[352,768]{1,0:T(8,128)(2,1)}, bf16[352,768]{1,0:T(8,128)(2,1)}, u32[]{:S(2)}, u32[]{:S(2)}) collective-permute-start(bf16[352,768]{1,0:T(8,128)(2,1)} %get-tuple-element.115), channel_id=1, source_target_pairs={{0,2},{1,0},{2,3},{3,1},{4,6},{5,4},{6,7},{7,5},{8,10},{9,8},{10,1... | collective-permute-start | bytes 1622024 | tf_op jit(solution)/shard_map/ppermute | solution.py:25
  61.4 55.7 %collective-permute-start.14 = (bf16[192,3072]{1,0:T(8,128)(2,1)}, bf16[192,3072]{1,0:T(8,128)(2,1)S(1)}, u32[]{:S(2)}, u32[]{:S(2)}) collective-permute-start(bf16[192,3072]{1,0:T(8,128)(2,1)} %param.39), channel_id=1, source_target_pairs={{0,2},{1,3},{2,0},{3,1},{4,6},{5,7},{6,4},{7,5},{8,10},{9,11},{10,... | collective-permute-start | bytes 3538952 | tf_op jit(solution)/shard_map/ppermute | solution.py:25
  67.4 76.2 %collective-permute-start.8 = (bf16[3,2,192,768]{3,2,1,0:T(8,128)(2,1)S(1)}, bf16[3,2,192,768]{3,2,1,0:T(8,128)(2,1)S(1)}, u32[]{:S(2)}, u32[]{:S(2)}) collective-permute-start(bf16[3,2,192,768]{3,2,1,0:T(8,128)(2,1)S(1)} %maximum_select_fusion.8), channel_id=1, source_target_pairs={{0,1},{1,0},{2,3},{3,2},{4,5},{5,4},{6,7},{7,6},{8,9},{9,8},{10,11... | collective-permute-start | bytes 5308424 | tf_op jit(solution)/shard_map/ppermute | solution.py:25
  80.4 61.5 %collective-permute-start.16 = (bf16[768,768]{1,0:T(8,128)(2,1)S(1)}, bf16[768,768]{1,0:T(8,128)(2,1)S(1)}, u32[]{:S(2)}, u32[]{:S(2)}) collective-permute-start(bf16[768,768]{1,0:T(8,128)(2,1)S(1)} %copy-done.16), channel_id=1, source_target_pairs={{0,2},{1,3},{2,0},{3,1},{4,6},{5,7},{6,4},{7,5},{8,10},{9,11},{10,... | collective-permute-start | bytes 3538952 | tf_op jit(solution)/shard_map/ppermute | solution.py:25
  117.1 33.9 %collective-permute-start.10 = (bf16[2,192,2304]{2,1,0:T(8,128)(2,1)S(1)}, bf16[2,192,2304]{2,1,0:T(8,128)(2,1)S(1)}, u32[]{:S(2)}, u32[]{:S(2)}) collective-permute-start(bf16[2,192,2304]{2,1,0:T(8,128)(2,1)S(1)} %maximum_select_fusion.10), channel_id=1, source_target_pairs={{0,1},{1,0},{2,3},{3,2},{4,5},{5,4},{6,7},{7,6},{8,9},{9,8},{10,11... | collective-permute-start | bytes 5308424 | tf_op jit(solution)/shard_map/ppermute | solution.py:25
  305.7 123.4 %collective-permute-start.18 = (bf16[352,768]{1,0:T(8,128)(2,1)}, bf16[352,768]{1,0:T(8,128)(2,1)}, u32[]{:S(2)}, u32[]{:S(2)}) collective-permute-start(bf16[352,768]{1,0:T(8,128)(2,1)} %get-tuple-element.116), channel_id=1, source_target_pairs={{0,0},{2,1},{1,2},{3,3},{4,4},{6,5},{5,6},{7,7},{8,8},{10,9},{9,10... | collective-permute-start | bytes 1622024 | tf_op jit(solution)/shard_map/ppermute | solution.py:25
  311.5 117.6 %collective-permute-start.19 = (bf16[352,768]{1,0:T(8,128)(2,1)}, bf16[352,768]{1,0:T(8,128)(2,1)}, u32[]{:S(2)}, u32[]{:S(2)}) collective-permute-start(bf16[352,768]{1,0:T(8,128)(2,1)} %get-tuple-element.117), channel_id=1, source_target_pairs={{2,0},{0,1},{3,2},{1,3},{6,4},{4,5},{7,6},{5,7},{10,8},{8,9},{11,1... | collective-permute-start | bytes 1622024 | tf_op jit(solution)/shard_map/ppermute | solution.py:25
  313.0 102.2 %collective-permute-start.52 = (bf16[2,192,768]{2,1,0:T(8,128)(2,1)}, bf16[2,192,768]{2,1,0:T(8,128)(2,1)}, u32[]{:S(2)}, u32[]{:S(2)}) collective-permute-start(bf16[2,192,768]{2,1,0:T(8,128)(2,1)} %convolution_convert_fusion.2), channel_id=1, source_target_pairs={{0,1},{1,0},{2,3},{3,2},{4,5},{5,4},{6,7},{7,6},{8,9},{9,8},{10,11... | collective-permute-start | bytes 1769480 | tf_op jit(solution)/shard_map/ppermute | solution.py:25
  365.2 68.8 %collective-permute-start.22 = (bf16[704,768]{1,0:T(8,128)(2,1)}, bf16[704,768]{1,0:T(8,128)(2,1)}, u32[]{:S(2)}, u32[]{:S(2)}) collective-permute-start(bf16[704,768]{1,0:T(8,128)(2,1)} %get-tuple-element.31), channel_id=1, source_target_pairs={{0,1},{1,0},{2,3},{3,2},{4,5},{5,4},{6,7},{7,6},{8,9},{9,8},{10,11... | collective-permute-start | bytes 3244040 | tf_op jit(solution)/shard_map/ppermute | solution.py:25
  429.1 206.3 %collective-permute-start.60 = (bf16[2,192,3072]{2,1,0:T(8,128)(2,1)}, bf16[2,192,3072]{2,1,0:T(8,128)(2,1)}, u32[]{:S(2)}, u32[]{:S(2)}) collective-permute-start(bf16[2,192,3072]{2,1,0:T(8,128)(2,1)} %fusion.9), channel_id=1, source_target_pairs={{0,1},{1,0},{2,3},{3,2},{4,5},{5,4},{6,7},{7,6},{8,9},{9,8},{10,11... | collective-permute-start | bytes 7077896 | tf_op jit(solution)/shard_map/ppermute | solution.py:25
  429.1 213.3 %collective-permute-start.68 = (bf16[2,768,768]{2,1,0:T(8,128)(2,1)}, bf16[2,768,768]{2,1,0:T(8,128)(2,1)}, u32[]{:S(2)}, u32[]{:S(2)}) collective-permute-start(bf16[2,768,768]{2,1,0:T(8,128)(2,1)} %fusion.45), channel_id=1, source_target_pairs={{0,1},{1,0},{2,3},{3,2},{4,5},{5,4},{6,7},{7,6},{8,9},{9,8},{10,11... | collective-permute-start | bytes 7077896 | tf_op jit(solution)/shard_map/ppermute | solution.py:25
  432.4 60.6 %collective-permute-start.55 = (bf16[48,768]{1,0:T(8,128)(2,1)S(1)}, bf16[48,768]{1,0:T(8,128)(2,1)S(1)}, u32[]{:S(2)}, u32[]{:S(2)}) collective-permute-start(bf16[48,768]{1,0:T(8,128)(2,1)S(1)} %dynamic-slice_bitcast_fusion.23), channel_id=1, source_target_pairs={{0,8},{4,12},{8,0},{12,4},{16,24},{20,28},{24,16},{28,20},{1,9},{5... | collective-permute-start | bytes 221192 | tf_op jit(solution)/shard_map/ppermute | solution.py:232
  492.1 126.6 %collective-permute-start.26 = (bf16[352,160]{1,0:T(8,128)(2,1)S(1)}, bf16[352,160]{1,0:T(8,128)(2,1)S(1)}, u32[]{:S(2)}, u32[]{:S(2)}) collective-permute-start(bf16[352,160]{1,0:T(8,128)(2,1)S(1)} %get-tuple-element.118), channel_id=1, source_target_pairs={{0,0},{2,1},{1,2},{3,3},{4,4},{6,5},{5,6},{7,7},{8,8},{10,9},{9,10... | collective-permute-start | bytes 337928 | tf_op jit(solution)/shard_map/ppermute | solution.py:25
  493.0 126.0 %collective-permute-start.27 = (bf16[352,160]{1,0:T(8,128)(2,1)S(1)}, bf16[352,160]{1,0:T(8,128)(2,1)S(1)}, u32[]{:S(2)}, u32[]{:S(2)}) collective-permute-start(bf16[352,160]{1,0:T(8,128)(2,1)S(1)} %get-tuple-element.119), channel_id=1, source_target_pairs={{2,0},{0,1},{3,2},{1,3},{6,4},{4,5},{7,6},{5,7},{10,8},{8,9},{11,1... | collective-permute-start | bytes 337928 | tf_op jit(solution)/shard_map/ppermute | solution.py:25
  503.7 98.2 %collective-permute-start.30 = (bf16[96,240]{1,0:T(8,128)(2,1)S(1)}, bf16[96,240]{1,0:T(8,128)(2,1)S(1)}, u32[]{:S(2)}, u32[]{:S(2)}) collective-permute-start(bf16[96,240]{1,0:T(8,128)(2,1)S(1)} %dynamic-slice_bitcast_fusion.24), channel_id=1, source_target_pairs={{0,4},{4,0},{8,12},{12,8},{16,20},{20,16},{24,28},{28,24},{1,5},{5... | collective-permute-start | bytes 138248 | tf_op jit(solution)/shard_map/ppermute | solution.py:232
  647.0 47.7 %collective-permute-start.69 = (bf16[768,768]{1,0:T(8,128)(2,1)S(1)}, bf16[768,768]{1,0:T(8,128)(2,1)S(1)}, u32[]{:S(2)}, u32[]{:S(2)}) collective-permute-start(bf16[768,768]{1,0:T(8,128)(2,1)S(1)} %dynamic-slice_bitcast_fusion), channel_id=1, source_target_pairs={{0,2},{1,3},{2,0},{3,1},{4,6},{5,7},{6,4},{7,5},{8,10},{9,11},{10,... | collective-permute-start | bytes 3538952 | tf_op jit(solution)/shard_map/ppermute | solution.py:25
  652.8 60.9 %collective-permute-start.45 = (bf16[192,2304]{1,0:T(8,128)(2,1)S(1)}, bf16[192,2304]{1,0:T(8,128)(2,1)S(1)}, u32[]{:S(2)}, u32[]{:S(2)}) collective-permute-start(bf16[192,2304]{1,0:T(8,128)(2,1)S(1)} %dynamic-slice_bitcast_fusion.2), channel_id=1, source_target_pairs={{0,2},{1,3},{2,0},{3,1},{4,6},{5,7},{6,4},{7,5},{8,10},{9,11},{10,... | collective-permute-start | bytes 2654216 | tf_op jit(solution)/shard_map/ppermute | solution.py:25
  655.9 75.5 %collective-permute-start.37 = (bf16[3,192,768]{2,1,0:T(8,128)(2,1)S(1)}, bf16[3,192,768]{2,1,0:T(8,128)(2,1)S(1)}, u32[]{:S(2)}, u32[]{:S(2)}) collective-permute-start(bf16[3,192,768]{2,1,0:T(8,128)(2,1)S(1)} %dynamic-slice_bitcast_fusion.3), channel_id=1, source_target_pairs={{0,2},{1,3},{2,0},{3,1},{4,6},{5,7},{6,4},{7,5},{8,10},{9,11},{10,... | collective-permute-start | bytes 2654216 | tf_op jit(solution)/shard_map/ppermute | solution.py:25
  669.9 63.5 %collective-permute-start.62 = (bf16[96,3072]{1,0:T(8,128)(2,1)S(1)}, bf16[96,3072]{1,0:T(8,128)(2,1)S(1)}, u32[]{:S(2)}, u32[]{:S(2)}) collective-permute-start(bf16[96,3072]{1,0:T(8,128)(2,1)S(1)} %dynamic-slice_bitcast_fusion.5), channel_id=1, source_target_pairs={{0,4},{4,0},{8,12},{12,8},{16,20},{20,16},{24,28},{28,24},{1,5},{5... | collective-permute-start | bytes 1769480 | tf_op jit(solution)/shard_map/ppermute | solution.py:232
  695.1 40.4 %collective-permute-start.70 = (bf16[384,768]{1,0:T(8,128)(2,1)S(1)}, bf16[384,768]{1,0:T(8,128)(2,1)S(1)}, u32[]{:S(2)}, u32[]{:S(2)}) collective-permute-start(bf16[384,768]{1,0:T(8,128)(2,1)S(1)} %dynamic-slice_bitcast_fusion.4), channel_id=1, source_target_pairs={{0,4},{4,0},{8,12},{12,8},{16,20},{20,16},{24,28},{28,24},{1,5},{5... | collective-permute-start | bytes 1769480 | tf_op jit(solution)/shard_map/ppermute | solution.py:232
  (144 other events, 1773.3 us)
Sparse Core Ops, SparseCore 0:
  480.8 117.5 all-reduce.2
